TPU v7x, 512 devices: a whole 4x4x16 slice. The times are simulated.
512 devices in a mesh: section: 16 (over y, x), expert: 32 (over z, core).
Axes of the slice: x: 4, y: 4, z: 16, core: 2. Of those that a mesh axis runs over, the one named last changes fastest.
Arguments:
- activations: bfloat16 [16, 4096, 2048], P('section', 'expert'), may hold values from -6 to 6
- norm_gain: float32 [16, 2048], P('section'), may hold values from 0.1 to 1.9
- router: bfloat16 [16, 2048, 8], P('section'), may hold values from -0.125 to 0.125
- expert_in: bfloat16 [16, 32, 2048, 512], P('section', 'expert'), may hold values from -0.125 to 0.125
- expert_down: bfloat16 [16, 32, 256, 2048], P('section', 'expert'), may hold values from -0.1875 to 0.1875
- expert_ids: int32 [2, 16, 4096], P(None, 'section', 'expert'), may hold values from 0 to 7, as said below
- slot_ids: int32 [2, 16, 4096], P(None, 'section', 'expert'), may hold values from 0 to 23, as said below
Outputs:
- carried: bfloat16 [16, 4096, 2048], P('section', 'expert')
Inputs may be any that keep to these rules, and one draw needn't show every extreme that they name: `expert_ids`: in each aligned block of 128 tokens at one stop and section, no two tokens share both expert and slot, and some expert has all 24 of its slots taken. `slot_ids`: slot of the token within the tile of its block and expert.
All inputs are finite; a program needn't handle non-finite values.
Results may differ from a plain program's by a relative error of at most 0.006.
Values may be sent and summed in bfloat16 or wider, within the bound.
A program may use at most 64 MiB of HBM per device.

v0:
```python
import jax
import jax.numpy as jnp
from jax import lax
from jax.sharding import PartitionSpec as P

SPLIT = 4
STEPS = 2


def shifted(block, axis, distance):
    devices = range(lax.axis_size(axis))
    route = [((i - distance) % len(devices), i) for i in devices]
    return lax.ppermute(block, axis, route)


def through_expert(row_block, gate_up, down_weight):
    hidden_width = down_weight.shape[0]
    projected = jnp.dot(row_block, gate_up, preferred_element_type=jnp.float32)
    hidden = (jax.nn.silu(projected[:, :hidden_width]) * projected[:, hidden_width:]).astype(
        jnp.bfloat16
    )
    return jnp.dot(hidden, down_weight, preferred_element_type=jnp.float32).astype(jnp.bfloat16)


def local(activations, norm_gain, router, expert_in, expert_down, expert_ids, slot_ids):
    experts = router.shape[2]
    tokens_here = activations.shape[1]
    model_width = activations.shape[2]
    devices = lax.axis_size("expert")
    capacity = SPLIT * (3 * tokens_here // (2 * experts * SPLIT))
    gate_up = expert_in[0, 0]
    down_weight = expert_down[0, 0]
    carried = activations
    for stop_index in range(STEPS):
        wide_rows = carried[0].astype(jnp.float32)
        inverse_rms = lax.rsqrt(jnp.mean(wide_rows * wide_rows, axis=-1, keepdims=True) + 1e-06)
        normed = (wide_rows * inverse_rms * norm_gain[0][None, :]).astype(jnp.bfloat16)
        logits = jnp.dot(normed, router[0], preferred_element_type=jnp.float32)
        chosen = expert_ids[stop_index, 0]
        picked = jnp.take_along_axis(logits, chosen[:, None], axis=1)
        weight = jax.nn.sigmoid(picked)
        target_row = chosen * capacity + slot_ids[stop_index, 0]
        expert_tiles = (
            jnp.zeros((experts * capacity, model_width), jnp.bfloat16).at[target_row].set(normed)
        )
        outgoing = jnp.repeat(expert_tiles.reshape(experts, capacity, model_width), SPLIT, axis=0)
        received = lax.all_to_all(outgoing, "expert", split_axis=0, concat_axis=0, tiled=True)
        slot_count = received.shape[1]
        partial_value = through_expert(received.reshape(-1, model_width), gate_up, down_weight)
        partial_value = partial_value.reshape(devices, slot_count, model_width)
        returned = lax.all_to_all(partial_value, "expert", split_axis=0, concat_axis=0, tiled=True)
        summed = jnp.sum(
            returned.reshape(experts, SPLIT, capacity, model_width).astype(jnp.float32), axis=1
        )
        expert_result = summed.astype(jnp.bfloat16).reshape(experts * capacity, model_width)
        gathered_rows = expert_result[target_row].astype(jnp.float32)
        mixed = (wide_rows + weight * gathered_rows).astype(jnp.bfloat16)
        carried = shifted(mixed[None], "section", 1)
    return carried


def solution(mesh):
    in_specs = (
        P("section", "expert", None),
        P("section", None),
        P("section", None, None),
        P("section", "expert", None, None),
        P("section", "expert", None, None),
        P(None, "section", "expert"),
        P(None, "section", "expert"),
    )
    out_specs = P("section", "expert", None)
    return jax.shard_map(local, mesh=mesh, in_specs=in_specs, out_specs=out_specs, check_vma=False)
```

profile of v0, /device:TPU:32, one launch (start us, length us, event | category | flops | bytes accessed | tf_op | source)
XLA Modules:
  0.0 675.8 jit_solution(12689109524493713972)
XLA Ops:
  0.0 1.4 fusion.11
  1.4 0.7 fusion.53
  2.1 2.2 scatter_custom_fusion
  4.3 0.4 broadcast_in_dim.7
  4.7 159.1 %all_to_all.20 = bf16[32,24,2048]{2,1,0:T(8,128)(2,1)S(1)} all-to-all(bf16[32,24,2048]{2,1,0:T(8,128)(2,1)S(1)} %bitcast.126), channel_id=1, replica_groups=mesh['section'=16,'expert'=32] {'expert'}, dimensions={0} | all-to-all | bytes 6291456 | tf_op jit(solution)/shard_map/all_to_all | solution.py:47
  163.9 1.8 fusion.2
  165.7 2.7 convolution_convert_fusion.1
  168.4 6.7 all-to-all-start.1
  175.1 0.3 fusion.28
  175.4 1.0 gather_fusion.2
  176.5 143.9 %all-to-all-done.1 = bf16[32,24,2048]{2,1,0:T(8,128)(2,1)} async-done(((bf16[32,24,2048]{2,1,0:T(8,128)(2,1)}), bf16[32,24,2048]{2,1,0:T(8,128)(2,1)}, u32[]{:S(2)}, u32[]{:S(2)}) %all-to-all-start.1) | async-done | bytes 3145760 | tf_op jit(solution)/shard_map/all_to_all | solution.py:51
  320.4 2.5 bitcast_reduce_fusion.1
  322.9 1.7 gather_fusion
  324.6 1.3 fusion.16
  325.9 3.4 collective-permute-start
  329.3 15.4 %collective-permute-done = bf16[1,128,2048]{2,1,0:T(8,128)(2,1)S(1)} collective-permute-done((bf16[1,128,2048]{2,1,0:T(8,128)(2,1)S(1)}, bf16[1,128,2048]{2,1,0:T(8,128)(2,1)S(1)}, u32[]{:S(2)}, u32[]{:S(2)}) %collective-permute-start) | collective-permute-done | bytes 524320 | tf_op jit(solution)/shard_map/ppermute | solution.py:13
  344.7 0.2 fusion.8
  344.9 1.7 scatter_custom_fusion.1
  346.6 0.4 broadcast_in_dim.8
  347.0 147.5 %all_to_all.21 = bf16[32,24,2048]{2,1,0:T(8,128)(2,1)S(1)} all-to-all(bf16[32,24,2048]{2,1,0:T(8,128)(2,1)S(1)} %bitcast.127), channel_id=1, replica_groups=mesh['section'=16,'expert'=32] {'expert'}, dimensions={0} | all-to-all | bytes 6291456 | tf_op jit(solution)/shard_map/all_to_all | solution.py:47
  494.5 1.8 fusion
  496.3 2.7 convolution_convert_fusion
  499.0 6.5 all-to-all-start.3
  505.6 0.3 fusion.25
  505.9 1.0 gather_fusion.3
  506.9 144.0 %all-to-all-done.3 = bf16[32,24,2048]{2,1,0:T(8,128)(2,1)} async-done(((bf16[32,24,2048]{2,1,0:T(8,128)(2,1)}), bf16[32,24,2048]{2,1,0:T(8,128)(2,1)}, u32[]{:S(2)}, u32[]{:S(2)}) %all-to-all-start.3) | async-done | bytes 3145760 | tf_op jit(solution)/shard_map/all_to_all | solution.py:51
  650.9 2.5 bitcast_reduce_fusion
  653.4 1.7 gather_fusion.1
  655.1 1.3 fusion.19
  656.4 1.9 collective-permute-start.1
  658.3 16.8 %collective-permute-done.1 = bf16[1,128,2048]{2,1,0:T(8,128)(2,1)S(1)} collective-permute-done((bf16[1,128,2048]{2,1,0:T(8,128)(2,1)S(1)}, bf16[1,128,2048]{2,1,0:T(8,128)(2,1)S(1)}, u32[]{:S(2)}, u32[]{:S(2)}) %collective-permute-start.1) | collective-permute-done | bytes 524320 | tf_op jit(solution)/shard_map/ppermute | solution.py:13
  675.1 0.8 copy.9
  (24 shorter events, 0.1 us)
Async XLA Ops:
  0.0 163.8 %copy-start = (bf16[1,1,2048,512]{3,2,1,0:T(8,128)(2,1)S(1)}, bf16[1,1,2048,512]{3,2,1,0:T(8,128)(2,1)}, u32[]{:S(2)}) copy-start(bf16[1,1,2048,512]{3,2,1,0:T(8,128)(2,1)} %param.12) | copy-start | bytes 6291460
  163.8 1.8 copy-start.4
  168.4 6.7 copy-start.1
  168.4 6.7 copy-start.2
  168.4 6.7 copy-start.6
  168.4 8.1 %copy-start.3 = (s32[2,1,128]{2,1,0:T(1,128)S(1)}, s32[2,1,128]{2,1,0:T(1,128)}, u32[]{:S(2)}) copy-start(s32[2,1,128]{2,1,0:T(1,128)} %param.14) | copy-start | bytes 3076
  168.4 152.0 %all-to-all-start.1 = ((bf16[32,24,2048]{2,1,0:T(8,128)(2,1)}), bf16[32,24,2048]{2,1,0:T(8,128)(2,1)}, u32[]{:S(2)}, u32[]{:S(2)}) async-start(bf16[32,24,2048]{2,1,0:T(8,128)(2,1)} %bitcast.128), calls=%async_computation.1 | async-start | bytes 6291456 | tf_op jit(solution)/shard_map/all_to_all | solution.py:51
  325.9 18.8 %collective-permute-start = (bf16[1,128,2048]{2,1,0:T(8,128)(2,1)S(1)}, bf16[1,128,2048]{2,1,0:T(8,128)(2,1)S(1)}, u32[]{:S(2)}, u32[]{:S(2)}) collective-permute-start(bf16[1,128,2048]{2,1,0:T(8,128)(2,1)S(1)} %fusion.16), channel_id=1, source_target_pairs={{480,0},{0,32},{32,64},{64,96},{96,128},{128,160},{160,192},{192,2... | collective-permute-start | bytes 1572872 | tf_op jit(solution)/shard_map/ppermute | solution.py:13
  494.5 1.8 copy-start.5
  499.0 151.9 %all-to-all-start.3 = ((bf16[32,24,2048]{2,1,0:T(8,128)(2,1)}), bf16[32,24,2048]{2,1,0:T(8,128)(2,1)}, u32[]{:S(2)}, u32[]{:S(2)}) async-start(bf16[32,24,2048]{2,1,0:T(8,128)(2,1)} %bitcast.129), calls=%async_computation.3 | async-start | bytes 6291456 | tf_op jit(solution)/shard_map/all_to_all | solution.py:51
  656.4 18.7 %collective-permute-start.1 = (bf16[1,128,2048]{2,1,0:T(8,128)(2,1)S(1)}, bf16[1,128,2048]{2,1,0:T(8,128)(2,1)S(1)}, u32[]{:S(2)}, u32[]{:S(2)}) collective-permute-start(bf16[1,128,2048]{2,1,0:T(8,128)(2,1)S(1)} %fusion.19), channel_id=1, source_target_pairs={{480,0},{0,32},{32,64},{64,96},{96,128},{128,160},{160,192},{192,2... | collective-permute-start | bytes 1572872 | tf_op jit(solution)/shard_map/ppermute | solution.py:13
where the time goes:
time: 676 us
  waiting for transfers between devices  320 us (47%)
  blocking collectives  307 us (45%)
  starting transfers between devices  18.5 us (3%)
  other arithmetic  13.7 us (2%)
  matrix products  9.64 us (1%)
  local copies, waits for them, and re-layouts  7.02 us (1%)
    all_to_all x2, blocking collectives, local(): lax.all_to_all(outgoing, 'expert', split_axis=0, concat_axis=0, tiled=True)  307 us
    all_to_all x2, waiting for transfers between devices, local(): lax.all_to_all(partial_value, 'expert', split_axis=0, concat_axis=0, tile...  288 us
    ppermute x2, waiting for transfers between devices, shifted(): return lax.ppermute(block, axis, route)  32.2 us
  transfers between devices with their start and end apart: 4, of which 4 were waited for; matrix products, arithmetic and copies ran while one was open for 0% of the time, Pallas kernels for 0%

commit v1 on v0

v1 whole, which is shorter than its diff:
```python
import functools

import jax
import jax.numpy as jnp
from jax import lax
from jax.experimental import pallas as pl
from jax.experimental.pallas import tpu as pltpu
from jax.sharding import PartitionSpec as P

STEPS = 2
CAP = 24
TOK = 128
SPLIT = 4
MESH = pl.DeviceIdType.MESH
LAND, TO_SIBLING, TO_PARTNER, TO_BOTH, PART_SIBLING, PART_FAR, PART_PARTNER, RESULT, META = range(9)


def kernel(
    n_section, n_expert,
    x_ref, gain_ref, router_ref, w_in_ref, w_down_ref, ids_ref, slots_ref,
    out_ref,
    x_buf, gain, router, w_in, w_down, ids, slots,
    normed, onehot, weight, onehot_in, weight_in, x_in,
    tiles, rows, part, far_in, sib_in, pair_in, pair_out, final, result,
    gathered, local_sem, send_sem, recv_sem,
):
    f32, bf16 = jnp.float32, jnp.bfloat16
    chips = n_expert // 2
    n_tiles = n_expert // SPLIT
    width = x_buf.shape[2]
    hidden_width = w_down.shape[0]
    s = lax.axis_index("section")
    e = lax.axis_index("expert")
    z, c = e // 2, e % 2
    side = z % 2
    s_next = (s + 1) % n_section
    s_prev = (s + n_section - 1) % n_section

    def source(k):
        return (z + (2 * side - 1) * k + chips) % chips

    def target(k):
        return (z + (1 - 2 * ((z + k) % 2)) * k + chips) % chips

    sibling = (s, e + 1 - 2 * c)
    partner = (s, (z + 1 - 2 * side) * 2 + c)

    loads = [
        pltpu.make_async_copy(x_ref.at[0], x_buf.at[0], local_sem.at[0]),
        pltpu.make_async_copy(gain_ref, gain, local_sem.at[1]),
        pltpu.make_async_copy(router_ref.at[0], router, local_sem.at[2]),
        pltpu.make_async_copy(ids_ref, ids, local_sem.at[3]),
        pltpu.make_async_copy(slots_ref, slots, local_sem.at[4]),
        pltpu.make_async_copy(w_in_ref.at[0, 0], w_in, local_sem.at[5]),
        pltpu.make_async_copy(w_down_ref.at[0, 0], w_down, local_sem.at[6]),
    ]
    for load in loads:
        load.start()

    barrier = pltpu.get_barrier_semaphore()

    def greet(device):
        pl.semaphore_signal(barrier, inc=1, device_id=device, device_id_type=MESH)

    greet(sibling)
    greet(partner)

    @pl.loop(0, n_tiles)
    def _(k):
        greet((s_next, source(k) * 2 + c))
        greet((s_prev, target(k) * 2 + c))

    @pl.loop(1, n_tiles)
    def _(k):
        greet((s, source(k) * 2 + c))
        greet((s, target(k) * 2 + c))

    for load in loads[:5]:
        load.wait()

    def remote(t, kind, k, src, dst, device):
        return pltpu.make_async_remote_copy(
            src_ref=src, dst_ref=dst, send_sem=send_sem.at[t, kind, k], recv_sem=recv_sem.at[t, kind, k],
            device_id=device, device_id_type=MESH,
        )

    def land(t, k):
        return remote(t, LAND, k, tiles.at[t, k], rows.at[t, 0, k], (s, target(k) * 2 + c))

    def to_sibling(t, k):
        return remote(t, TO_SIBLING, k, rows.at[t, 0, k], rows.at[t, 1, k], sibling)

    def to_partner(t, k):
        return remote(t, TO_PARTNER, k, rows.at[t, 0, k], rows.at[t, 2, k], partner)

    def to_both(t, k):
        return remote(t, TO_BOTH, k, rows.at[t, 2, k], rows.at[t, 3, k], sibling)

    def part_sibling(t, k):
        return remote(t, PART_SIBLING, k, part.at[t, 1, k], sib_in.at[t, k], sibling)

    def part_far(t, k):
        return remote(t, PART_FAR, k, part.at[t, 3, k], far_in.at[t, k], sibling)

    def part_partner(t, k):
        return remote(t, PART_PARTNER, k, pair_out.at[t, k], pair_in.at[t, k], partner)

    def to_home(t, k):
        return remote(t, RESULT, k, final.at[t, k], result.at[t, k], (s_next, source(k) * 2 + c))

    def metas(t):
        home = (s_next, e)
        return (
            remote(t, META, 0, x_buf.at[t], x_in.at[t], home),
            remote(t, META, 1, weight.at[t], weight_in.at[t], home),
            remote(t, META, 2, onehot.at[t], onehot_in.at[t], home),
        )

    def norm_and_route(t):
        @pl.loop(0, TOK // 16)
        def _(i):
            at = pl.ds(pl.multiple_of(i * 16, 16), 16)
            wide = x_buf[t, at, :].astype(f32)
            inverse = lax.rsqrt(jnp.mean(wide * wide, axis=-1, keepdims=True) + 1e-06)
            normed[at, :] = (wide * inverse * gain[...]).astype(bf16)

        id_row = ids[t]
        row_of = id_row * CAP + slots[t]
        for k in range(n_tiles):
            owner = target(k) // 2
            place = lax.broadcasted_iota(jnp.int32, (CAP, TOK), 0) + owner * CAP
            hot = jnp.where(place == row_of, 1.0, 0.0)
            onehot[t, k] = hot.astype(bf16)

        @pl.loop(0, n_tiles)
        def _(k):
            tile = jnp.dot(onehot[t, k], normed[...], preferred_element_type=f32).astype(bf16)

            @pl.when(k == 0)
            def _():
                rows[t, 0, 0] = tile

            @pl.when(k > 0)
            def _():
                tiles[t, k] = tile

            @pl.when((k == 0) & (t == 0))
            def _():
                pl.semaphore_wait(barrier, 4 * n_tiles)

            @pl.when(k > 0)
            def _():
                land(t, k).start()

        logits = jnp.dot(normed[...], router[...], preferred_element_type=f32)
        id_column = jnp.transpose(jnp.broadcast_to(id_row.astype(f32), (TOK, TOK)))[:, : logits.shape[1]]
        lanes = lax.broadcasted_iota(jnp.int32, logits.shape, 1)
        picked = jnp.sum(jnp.where(id_column.astype(jnp.int32) == lanes, logits, 0.0), axis=1, keepdims=True)
        weight[t] = jnp.broadcast_to(jax.nn.sigmoid(picked), (TOK, TOK))
        for copy in metas(t):
            copy.start()

    def experts(t, k):
        held = jnp.concatenate([rows[t, g, k].astype(f32) for g in range(SPLIT)], axis=0).astype(bf16)
        projected = jnp.dot(held, w_in[...], preferred_element_type=f32)
        gate, up = projected[:, :hidden_width], projected[:, hidden_width:]
        hidden = (gate * jax.nn.sigmoid(gate) * up).astype(bf16)
        value = jnp.dot(hidden, w_down[...], preferred_element_type=f32)
        for g in range(SPLIT):
            part[t, g, k] = value[g * CAP : (g + 1) * CAP].astype(bf16)

    def stop(t):
        norm_and_route(t)
        if t == 0:
            for load in loads[5:]:
                load.wait()

        @pl.loop(0, n_tiles + 4)
        def _(i):
            @pl.when(i < n_tiles)
            def _():
                @pl.when(i > 0)
                def _():
                    land(t, i).wait_recv()

                to_partner(t, i).start()
                to_sibling(t, i).start()

            @pl.when((i >= 1) & (i < n_tiles + 1))
            def _():
                k = i - 1
                to_partner(t, k).wait_recv()
                to_both(t, k).start()

            @pl.when((i >= 2) & (i < n_tiles + 2))
            def _():
                k = i - 2
                to_sibling(t, k).wait_recv()
                to_both(t, k).wait_recv()
                experts(t, k)
                part_far(t, k).start()
                part_sibling(t, k).start()

            @pl.when((i >= 3) & (i < n_tiles + 3))
            def _():
                k = i - 3
                part_far(t, k).wait_recv()
                pair_out[t, k] = (part[t, 2, k].astype(f32) + far_in[t, k].astype(f32)).astype(bf16)
                part_partner(t, k).start()

            @pl.when(i >= 4)
            def _():
                k = i - 4
                part_sibling(t, k).wait_recv()
                part_partner(t, k).wait_recv()
                total = part[t, 0, k].astype(f32) + sib_in[t, k].astype(f32) + pair_in[t, k].astype(f32)
                final[t, k] = total.astype(bf16)
                to_home(t, k).start()

        for copy in metas(t):
            copy.wait_recv()

        @pl.loop(0, n_tiles)
        def _(k):
            to_home(t, k).wait_recv()
            here = lax.dot_general(
                onehot_in[t, k], result[t, k], (((0,), (0,)), ((), ())), preferred_element_type=f32
            )

            @pl.when(k == 0)
            def _():
                gathered[...] = here

            @pl.when(k > 0)
            def _():
                gathered[...] += here

        @pl.loop(0, TOK // 16)
        def _(i):
            at = pl.ds(pl.multiple_of(i * 16, 16), 16)
            mixed = x_in[t, at, :].astype(f32) + weight_in[t, at, 0:1] * gathered[at, :]
            x_buf[t + 1, at, :] = mixed.astype(bf16)

    for t in range(STEPS):
        stop(t)
    store = pltpu.make_async_copy(x_buf.at[STEPS], out_ref.at[0], local_sem.at[0])
    store.start()
    for t in range(STEPS):
        for copy in metas(t):
            copy.wait_send()

        @pl.loop(0, n_tiles)
        def _(k):
            @pl.when(k > 0)
            def _():
                land(t, k).wait_send()

            for copy in (to_sibling, to_partner, to_both, part_sibling, part_far, part_partner, to_home):
                copy(t, k).wait_send()

    store.wait()


def local(n_section, n_expert, activations, norm_gain, router, expert_in, expert_down, expert_ids, slot_ids):
    width = activations.shape[2]
    experts = router.shape[2]
    n_tiles = n_expert // SPLIT
    bf16, f32 = jnp.bfloat16, jnp.float32
    tile_set = (STEPS, n_tiles, CAP, width)
    vmem = pltpu.VMEM
    return pl.pallas_call(
        functools.partial(kernel, n_section, n_expert),
        out_shape=jax.ShapeDtypeStruct(activations.shape, bf16),
        in_specs=[pl.BlockSpec(memory_space=pl.ANY)] * 7,
        out_specs=pl.BlockSpec(memory_space=pl.ANY),
        scratch_shapes=[
            vmem((STEPS + 1, TOK, width), bf16),
            vmem((1, width), f32),
            vmem((width, experts), bf16),
            vmem(expert_in.shape[2:], bf16),
            vmem(expert_down.shape[2:], bf16),
            vmem(expert_ids.shape, jnp.int32),
            vmem(slot_ids.shape, jnp.int32),
            vmem((TOK, width), bf16),
            vmem((STEPS, n_tiles, CAP, TOK), bf16),
            vmem((STEPS, TOK, TOK), f32),
            vmem((STEPS, n_tiles, CAP, TOK), bf16),
            vmem((STEPS, TOK, TOK), f32),
            vmem((STEPS, TOK, width), bf16),
            vmem(tile_set, bf16),
            vmem((STEPS, SPLIT, n_tiles, CAP, width), bf16),
            vmem((STEPS, SPLIT, n_tiles, CAP, width), bf16),
            vmem(tile_set, bf16),
            vmem(tile_set, bf16),
            vmem(tile_set, bf16),
            vmem(tile_set, bf16),
            vmem(tile_set, bf16),
            vmem(tile_set, bf16),
            vmem((TOK, width), f32),
            pltpu.SemaphoreType.DMA((7,)),
            pltpu.SemaphoreType.DMA((STEPS, 9, n_tiles)),
            pltpu.SemaphoreType.DMA((STEPS, 9, n_tiles)),
        ],
        compiler_params=pltpu.CompilerParams(
            collective_id=0, has_side_effects=True, vmem_limit_bytes=58 * 1024 * 1024
        ),
        cost_estimate=pl.CostEstimate(flops=5_000_000_000, bytes_accessed=5_000_000, transcendentals=800_000),
    )(activations, norm_gain, router, expert_in, expert_down, expert_ids, slot_ids)


def solution(mesh):
    in_specs = (
        P("section", "expert", None),
        P("section", None),
        P("section", None, None),
        P("section", "expert", None, None),
        P("section", "expert", None, None),
        P(None, "section", "expert"),
        P(None, "section", "expert"),
    )
    body = functools.partial(local, mesh.shape["section"], mesh.shape["expert"])
    return jax.shard_map(body, mesh=mesh, in_specs=in_specs, out_specs=P("section", "expert", None), check_vma=False)
```

time: 676 us -> 222 us (0.33)
  the two profiles are of different devices: /device:TPU:32 before, /device:TPU:26 now
where the time goes in v1:
time: 222 us
  Pallas kernels  218 us (98%)
  local copies, waits for them, and re-layouts  3.64 us (2%)
    pallas_call x1, Pallas kernels, local(): pl.pallas_call(functools.partial(kernel, n_section, n_expert), out_shape=...  218 us

profile of v1, /device:TPU:26, one launch (start us, length us, event | category | flops | bytes accessed | tf_op | source)
XLA Modules:
  0.0 222.1 jit_solution(9732786470317462485)
XLA Ops:
  0.0 1.8 copy.8.router_ref
  1.8 218.4 %shard_map.73 = bf16[1,128,2048]{2,1,0:T(8,128)(2,1)} custom-call(bf16[1,128,2048]{2,1,0:T(8,128)(2,1)} %x_ref.1, f32[1,2048]{1,0:T(1,128)} %gain_ref.1, bf16[1,2048,8]{2,1,0:T(8,128)(2,1)} %copy.8.router_ref, bf16[1,1,2048,512]{3,2,1,0:T(8,128)(2,1)} %w_in_ref.1, bf16[1,1,256,2048]{3,2,1,0:T(8,128)(2,1)} %w_down_ref.1, s32[2,1,128]{2,1,0:T(1,128)} %ids_ref.1, ...), custom_call_target="tpu_custom_call" | custom-call | flops 5000000000 | bytes 5000000 | tf_op jit(solution)/shard_map/pallas_call | solution.py:271
  220.2 1.9 copy.10

commit v2 on v1

v2 whole, which is shorter than its diff:
```python
import functools

import jax
import jax.numpy as jnp
from jax import lax
from jax.experimental import pallas as pl
from jax.experimental.pallas import tpu as pltpu
from jax.sharding import PartitionSpec as P

STEPS = 2
PAIR = 2
OFFSET = 4
ORDER = "ABSCDEG"
CAP = 24
TOK = 128
SPLIT = 4
MESH = pl.DeviceIdType.MESH
LAND, TO_SIBLING, TO_PARTNER, TO_BOTH, PART_SIBLING, PART_FAR, PART_PARTNER, RESULT, META = range(9)


def kernel(
    n_section, n_expert,
    x_ref, gain_ref, router_ref, w_in_ref, w_down_ref, ids_ref, slots_ref,
    out_ref,
    x_buf, gain, router, w_in, w_down, ids, slots,
    normed, onehot, weight, onehot_in, weight_in, x_in,
    tiles, rows, part, far_in, sib_in, pair_in, pair_out, final, result,
    gathered, local_sem, send_sem, recv_sem,
):
    f32, bf16 = jnp.float32, jnp.bfloat16
    chips = n_expert // 2
    n_tiles = n_expert // SPLIT
    width = x_buf.shape[2]
    hidden_width = w_down.shape[0]
    s = lax.axis_index("section")
    e = lax.axis_index("expert")
    z, c = e // 2, e % 2
    side = z % 2
    s_next = (s + 1) % n_section
    s_prev = (s + n_section - 1) % n_section

    def source(k):
        return (z + (2 * side - 1) * k + chips) % chips

    def target(k):
        return (z + (1 - 2 * ((z + k) % 2)) * k + chips) % chips

    sibling = (s, e + 1 - 2 * c)
    partner = (s, (z + 1 - 2 * side) * 2 + c)

    loads = [
        pltpu.make_async_copy(x_ref.at[0], x_buf.at[0], local_sem.at[0]),
        pltpu.make_async_copy(gain_ref, gain, local_sem.at[1]),
        pltpu.make_async_copy(router_ref.at[0], router, local_sem.at[2]),
        pltpu.make_async_copy(ids_ref, ids, local_sem.at[3]),
        pltpu.make_async_copy(slots_ref, slots, local_sem.at[4]),
        pltpu.make_async_copy(w_in_ref.at[0, 0], w_in, local_sem.at[5]),
        pltpu.make_async_copy(w_down_ref.at[0, 0], w_down, local_sem.at[6]),
    ]
    for load in loads:
        load.start()

    barrier = pltpu.get_barrier_semaphore()

    def greet(device):
        pl.semaphore_signal(barrier, inc=1, device_id=device, device_id_type=MESH)

    greet(sibling)
    greet(partner)

    @pl.loop(0, n_tiles)
    def _(k):
        greet((s_next, source(k) * 2 + c))
        greet((s_prev, target(k) * 2 + c))

    @pl.loop(1, n_tiles)
    def _(k):
        greet((s, source(k) * 2 + c))
        greet((s, target(k) * 2 + c))

    for load in loads[:5]:
        load.wait()

    groups = n_tiles // PAIR
    period = groups + 6

    def some(q):
        return pl.ds(q * PAIR, PAIR)

    def remote(t, kind, k, src, dst, device):
        return pltpu.make_async_remote_copy(
            src_ref=src, dst_ref=dst, send_sem=send_sem.at[t, kind, k], recv_sem=recv_sem.at[t, kind, k],
            device_id=device, device_id_type=MESH,
        )

    def land(t, k):
        return remote(t, LAND, k, tiles.at[t, k], rows.at[t, 0, k], (s, target(k) * 2 + c))

    def to_sibling(t, q):
        return remote(t, TO_SIBLING, q, rows.at[t, 0, some(q)], rows.at[t, 1, some(q)], sibling)

    def to_partner(t, q):
        return remote(t, TO_PARTNER, q, rows.at[t, 0, some(q)], rows.at[t, 2, some(q)], partner)

    def to_both(t, q):
        return remote(t, TO_BOTH, q, rows.at[t, 2, some(q)], rows.at[t, 3, some(q)], sibling)

    def part_sibling(t, q):
        return remote(t, PART_SIBLING, q, part.at[t, 1, some(q)], sib_in.at[t, some(q)], sibling)

    def part_far(t, q):
        return remote(t, PART_FAR, q, part.at[t, 3, some(q)], far_in.at[t, some(q)], sibling)

    def part_partner(t, q):
        return remote(t, PART_PARTNER, q, pair_out.at[t, some(q)], pair_in.at[t, some(q)], partner)

    def to_home(t, k):
        return remote(t, RESULT, k, final.at[t, k], result.at[t, k], (s_next, source(k) * 2 + c))

    def meta(t, which):
        src, dst = ((x_buf, x_in), (weight, weight_in), (onehot, onehot_in))[which]
        return remote(t, META, which, src.at[t], dst.at[t], (s_next, e))

    def prepare(t):
        for i in range(TOK // 16):
            at = pl.ds(i * 16, 16)
            wide = x_buf[t, at, :].astype(f32)
            inverse = lax.rsqrt(jnp.mean(wide * wide, axis=-1, keepdims=True) + 1e-06)
            normed[at, :] = (wide * inverse * gain[...]).astype(bf16)

        row_of = ids[t] * CAP + slots[t]
        for k in range(n_tiles):
            place = lax.broadcasted_iota(jnp.int32, (CAP, TOK), 0) + (target(k) // 2) * CAP
            onehot[t, k] = jnp.where(place == row_of, 1.0, 0.0).astype(bf16)

    def dispatch(t):
        def scattered(k):
            return jnp.dot(onehot[t, k], normed[...], preferred_element_type=f32).astype(bf16)

        @pl.loop(1, n_tiles)
        def _(k):
            tiles[t, k] = scattered(k)
            land(t, k).start()

        rows[t, 0, 0] = scattered(0)

        logits = lax.dot_general(
            router[...], normed[...], (((1,), (1,)), ((), ())), preferred_element_type=f32
        )
        expert = lax.broadcasted_iota(jnp.int32, logits.shape, 0)
        picked = jnp.sum(jnp.where(expert == ids[t], logits, 0.0), axis=0, keepdims=True)
        weight[t] = jnp.transpose(jnp.broadcast_to(jax.nn.sigmoid(picked), (TOK, TOK)))
        for which in range(3):
            meta(t, which).start()

    def experts(t, members, q):
        held = jnp.concatenate(
            [rows[t, g, q * PAIR + a].astype(f32) for g in members for a in range(PAIR)], axis=0
        ).astype(bf16)
        projected = jnp.dot(held, w_in[...], preferred_element_type=f32)
        gate, up = projected[:, :hidden_width], projected[:, hidden_width:]
        hidden = (gate * jax.nn.sigmoid(gate) * up).astype(bf16)
        value = jnp.dot(hidden, w_down[...], preferred_element_type=f32)
        at = 0
        for g in members:
            for a in range(PAIR):
                part[t, g, q * PAIR + a] = value[at : at + CAP].astype(bf16)
                at += CAP

    def mix(t):
        for which in range(2):
            meta(t, which).wait_recv()
        for i in range(TOK // 16):
            at = pl.ds(i * 16, 16)
            mixed = x_in[t, at, :].astype(f32) + weight_in[t, at, 0:1] * gathered[at, :]
            x_buf[t + 1, at, :] = mixed.astype(bf16)

    def hand_on(t, q):
        for a in range(PAIR):
            k = q * PAIR + a

            @pl.when(k > 0)
            def _():
                land(t, k).wait_recv()

        to_partner(t, q).start()
        to_sibling(t, q).start()

    def hand_over(t, q):
        to_partner(t, q).wait_recv()
        to_both(t, q).start()

    def own_experts(t, q):
        experts(t, (0, 2), q)

    def sibling_experts(t, q):
        to_sibling(t, q).wait_recv()
        to_both(t, q).wait_recv()
        experts(t, (1, 3), q)
        part_far(t, q).start()
        part_sibling(t, q).start()

    def add_pair(t, q):
        part_far(t, q).wait_recv()
        for a in range(PAIR):
            k = q * PAIR + a
            pair_out[t, k] = (part[t, 2, k].astype(f32) + far_in[t, k].astype(f32)).astype(bf16)
        part_partner(t, q).start()

    def add_all(t, q):
        part_sibling(t, q).wait_recv()
        part_partner(t, q).wait_recv()
        for a in range(PAIR):
            k = q * PAIR + a
            total = part[t, 0, k].astype(f32) + sib_in[t, k].astype(f32) + pair_in[t, k].astype(f32)
            final[t, k] = total.astype(bf16)
            to_home(t, k).start()

    def gather(t, q):
        for a in range(PAIR):
            k = q * PAIR + a
            to_home(t, k).wait_recv()
            here = lax.dot_general(
                onehot_in[t, k], result[t, k], (((0,), (0,)), ((), ())), preferred_element_type=f32
            )
            if a == 0:
                @pl.when(k == 0)
                def _():
                    gathered[...] = here

                @pl.when(k > 0)
                def _():
                    gathered[...] += here
            else:
                gathered[...] += here

    own_turn = {
        "A": (hand_on, 0), "B": (hand_over, 1), "C": (own_experts, 2), "D": (add_pair, 3), "E": (add_all, 4),
        "G": (gather, 6),
    }

    prepare(0)
    for load in loads[5:]:
        load.wait()
    pl.semaphore_wait(barrier, 4 * n_tiles)

    @pl.loop(0, STEPS * period + OFFSET + 1)
    def _(turn):
        own = turn - 1 - c * OFFSET
        other = turn - 1 - (1 - c) * OFFSET

        def at_turn(action, index, delay):
            later = index + period
            t = later // period - 1
            q = later % period - delay

            @pl.when((index >= 0) & (t < STEPS) & (q >= 0) & (q < groups))
            def _():
                action(jnp.minimum(jnp.maximum(t, 0), STEPS - 1), jnp.minimum(jnp.maximum(q, 0), groups - 1))

        for name in ORDER:
            if name == "S":
                at_turn(sibling_experts, other, 2)
            else:
                action, delay = own_turn[name]
                if name == "G":
                    @pl.when((own >= 0) & (own < STEPS * period) & (own % period == 6))
                    def _():
                        meta(jnp.minimum(own // period, STEPS - 1), 2).wait_recv()

                at_turn(action, own, delay)

        upcoming = (own + 1 + period) // period - 1

        @pl.when((own >= 0) & (own % period == period - 1) & (upcoming <= STEPS))
        def _():
            mix(jnp.minimum(jnp.maximum(upcoming - 1, 0), STEPS - 1))

        @pl.when((own >= 0) & (own % period == period - 1) & (upcoming < STEPS))
        def _():
            prepare(jnp.minimum(jnp.maximum(upcoming, 0), STEPS - 1))

        @pl.when((own >= -1) & ((own + 1) % period == 0) & (upcoming < STEPS))
        def _():
            dispatch(jnp.minimum(jnp.maximum(upcoming, 0), STEPS - 1))

    store = pltpu.make_async_copy(x_buf.at[STEPS], out_ref.at[0], local_sem.at[0])
    store.start()

    @pl.loop(0, STEPS)
    def _(t):
        for which in range(3):
            meta(t, which).wait_send()

        @pl.loop(0, n_tiles)
        def _(k):
            @pl.when(k > 0)
            def _():
                land(t, k).wait_send()

            to_home(t, k).wait_send()

        @pl.loop(0, groups)
        def _(q):
            for copy in (to_sibling, to_partner, to_both, part_sibling, part_far, part_partner):
                copy(t, q).wait_send()

    store.wait()


def local(n_section, n_expert, activations, norm_gain, router, expert_in, expert_down, expert_ids, slot_ids):
    width = activations.shape[2]
    experts = router.shape[2]
    n_tiles = n_expert // SPLIT
    bf16, f32 = jnp.bfloat16, jnp.float32
    tile_set = (STEPS, n_tiles, CAP, width)
    vmem = pltpu.VMEM
    return pl.pallas_call(
        functools.partial(kernel, n_section, n_expert),
        out_shape=jax.ShapeDtypeStruct(activations.shape, bf16),
        in_specs=[pl.BlockSpec(memory_space=pl.ANY)] * 7,
        out_specs=pl.BlockSpec(memory_space=pl.ANY),
        scratch_shapes=[
            vmem((STEPS + 1, TOK, width), bf16),
            vmem((1, width), f32),
            vmem((experts, width), bf16),
            vmem(expert_in.shape[2:], bf16),
            vmem(expert_down.shape[2:], bf16),
            vmem(expert_ids.shape, jnp.int32),
            vmem(slot_ids.shape, jnp.int32),
            vmem((TOK, width), bf16),
            vmem((STEPS, n_tiles, CAP, TOK), bf16),
            vmem((STEPS, TOK, TOK), f32),
            vmem((STEPS, n_tiles, CAP, TOK), bf16),
            vmem((STEPS, TOK, TOK), f32),
            vmem((STEPS, TOK, width), bf16),
            vmem(tile_set, bf16),
            vmem((STEPS, SPLIT, n_tiles, CAP, width), bf16),
            vmem((STEPS, SPLIT, n_tiles, CAP, width), bf16),
            vmem(tile_set, bf16),
            vmem(tile_set, bf16),
            vmem(tile_set, bf16),
            vmem(tile_set, bf16),
            vmem(tile_set, bf16),
            vmem(tile_set, bf16),
            vmem((TOK, width), f32),
            pltpu.SemaphoreType.DMA((7,)),
            pltpu.SemaphoreType.DMA((STEPS, 9, n_tiles)),
            pltpu.SemaphoreType.DMA((STEPS, 9, n_tiles)),
        ],
        compiler_params=pltpu.CompilerParams(
            collective_id=0, has_side_effects=True, vmem_limit_bytes=58 * 1024 * 1024
        ),
        cost_estimate=pl.CostEstimate(flops=5_000_000_000, bytes_accessed=5_000_000, transcendentals=800_000),
    )(activations, norm_gain, jnp.swapaxes(router, 1, 2), expert_in, expert_down, expert_ids, slot_ids)


def solution(mesh):
    in_specs = (
        P("section", "expert", None),
        P("section", None),
        P("section", None, None),
        P("section", "expert", None, None),
        P("section", "expert", None, None),
        P(None, "section", "expert"),
        P(None, "section", "expert"),
    )
    body = functools.partial(local, mesh.shape["section"], mesh.shape["expert"])
    return jax.shard_map(body, mesh=mesh, in_specs=in_specs, out_specs=P("section", "expert", None), check_vma=False)
```

time: 222 us -> 213 us (0.959)
  the two profiles are of different devices: /device:TPU:26 before, /device:TPU:3 now
where the time goes in v2:
time: 213 us
  Pallas kernels  211 us (99%)
    pallas_call x1, Pallas kernels, local(): pl.pallas_call(functools.partial(kernel, n_section, n_expert), out_shape=...  211 us

profile of v2, /device:TPU:3, one launch (start us, length us, event | category | flops | bytes accessed | tf_op | source)
XLA Modules:
  0.0 213.2 jit_solution(1704707453879347386)
XLA Ops:
  0.0 211.3 %shard_map.73 = bf16[1,128,2048]{2,1,0:T(8,128)(2,1)} custom-call(bf16[1,128,2048]{2,1,0:T(8,128)(2,1)} %x_ref.1, f32[1,2048]{1,0:T(1,128)} %gain_ref.1, bf16[1,8,2048]{2,1,0:T(8,128)(2,1)} %bitcast.1, bf16[1,1,2048,512]{3,2,1,0:T(8,128)(2,1)} %w_in_ref.1, bf16[1,1,256,2048]{3,2,1,0:T(8,128)(2,1)} %w_down_ref.1, s32[2,1,128]{2,1,0:T(1,128)} %ids_ref.1, ...), custom_call_target="tpu_custom_call" | custom-call | flops 5000000000 | bytes 5000000 | tf_op jit(solution)/shard_map/pallas_call | solution.py:318
  211.3 1.9 copy.9

commit v3 on v2

--- a/solution.py
+++ b/solution.py
@@ -9,8 +9,9 @@
 
 STEPS = 2
 PAIR = 2
-OFFSET = 4
-ORDER = "ABSCDEG"
+OFFSET = 5
+TURN = {"A": 0, "B": 1, "S": 2, "C": 2, "D": 3, "E": 5, "G": 7}
+ORDER = "ADBSCEG"
 CAP = 24
 TOK = 128
 SPLIT = 4
@@ -57,7 +58,7 @@
         pltpu.make_async_copy(w_in_ref.at[0, 0], w_in, local_sem.at[5]),
         pltpu.make_async_copy(w_down_ref.at[0, 0], w_down, local_sem.at[6]),
     ]
-    for load in loads:
+    for load in loads[:5]:
         load.start()
 
     barrier = pltpu.get_barrier_semaphore()
@@ -80,12 +81,11 @@
 
     for load in loads[:5]:
         load.wait()
+    for load in loads[5:]:
+        load.start()
 
     groups = n_tiles // PAIR
-    period = groups + 6
-
-    def some(q):
-        return pl.ds(q * PAIR, PAIR)
+    period = groups + TURN["G"]
 
     def remote(t, kind, k, src, dst, device):
         return pltpu.make_async_remote_copy(
@@ -96,23 +96,23 @@
     def land(t, k):
         return remote(t, LAND, k, tiles.at[t, k], rows.at[t, 0, k], (s, target(k) * 2 + c))
 
-    def to_sibling(t, q):
-        return remote(t, TO_SIBLING, q, rows.at[t, 0, some(q)], rows.at[t, 1, some(q)], sibling)
-
-    def to_partner(t, q):
-        return remote(t, TO_PARTNER, q, rows.at[t, 0, some(q)], rows.at[t, 2, some(q)], partner)
-
-    def to_both(t, q):
-        return remote(t, TO_BOTH, q, rows.at[t, 2, some(q)], rows.at[t, 3, some(q)], sibling)
-
-    def part_sibling(t, q):
-        return remote(t, PART_SIBLING, q, part.at[t, 1, some(q)], sib_in.at[t, some(q)], sibling)
-
-    def part_far(t, q):
-        return remote(t, PART_FAR, q, part.at[t, 3, some(q)], far_in.at[t, some(q)], sibling)
-
-    def part_partner(t, q):
-        return remote(t, PART_PARTNER, q, pair_out.at[t, some(q)], pair_in.at[t, some(q)], partner)
+    def to_sibling(t, k):
+        return remote(t, TO_SIBLING, k, rows.at[t, 0, k], rows.at[t, 1, k], sibling)
+
+    def to_partner(t, k):
+        return remote(t, TO_PARTNER, k, rows.at[t, 0, k], rows.at[t, 2, k], partner)
+
+    def to_both(t, k):
+        return remote(t, TO_BOTH, k, rows.at[t, 2, k], rows.at[t, 3, k], sibling)
+
+    def part_sibling(t, k):
+        return remote(t, PART_SIBLING, k, part.at[t, 1, k], sib_in.at[t, k], sibling)
+
+    def part_far(t, k):
+        return remote(t, PART_FAR, k, part.at[t, 3, k], far_in.at[t, k], sibling)
+
+    def part_partner(t, k):
+        return remote(t, PART_PARTNER, k, pair_out.at[t, k], pair_in.at[t, k], partner)
 
     def to_home(t, k):
         return remote(t, RESULT, k, final.at[t, k], result.at[t, k], (s_next, source(k) * 2 + c))
@@ -183,35 +183,39 @@
             def _():
                 land(t, k).wait_recv()
 
-        to_partner(t, q).start()
-        to_sibling(t, q).start()
+            to_partner(t, k).start()
+            to_sibling(t, k).start()
 
     def hand_over(t, q):
-        to_partner(t, q).wait_recv()
-        to_both(t, q).start()
+        for a in range(PAIR):
+            k = q * PAIR + a
+            to_partner(t, k).wait_recv()
+            to_both(t, k).start()
 
     def own_experts(t, q):
         experts(t, (0, 2), q)
 
     def sibling_experts(t, q):
-        to_sibling(t, q).wait_recv()
-        to_both(t, q).wait_recv()
+        for a in range(PAIR):
+            to_sibling(t, q * PAIR + a).wait_recv()
+            to_both(t, q * PAIR + a).wait_recv()
         experts(t, (1, 3), q)
-        part_far(t, q).start()
-        part_sibling(t, q).start()
+        for copy in (part_far, part_sibling):
+            for a in range(PAIR):
+                copy(t, q * PAIR + a).start()
 
     def add_pair(t, q):
-        part_far(t, q).wait_recv()
-        for a in range(PAIR):
-            k = q * PAIR + a
+        for a in range(PAIR):
+            k = q * PAIR + a
+            part_far(t, k).wait_recv()
             pair_out[t, k] = (part[t, 2, k].astype(f32) + far_in[t, k].astype(f32)).astype(bf16)
-        part_partner(t, q).start()
+            part_partner(t, k).start()
 
     def add_all(t, q):
-        part_sibling(t, q).wait_recv()
-        part_partner(t, q).wait_recv()
-        for a in range(PAIR):
-            k = q * PAIR + a
+        for a in range(PAIR):
+            k = q * PAIR + a
+            part_sibling(t, k).wait_recv()
+            part_partner(t, k).wait_recv()
             total = part[t, 0, k].astype(f32) + sib_in[t, k].astype(f32) + pair_in[t, k].astype(f32)
             final[t, k] = total.astype(bf16)
             to_home(t, k).start()
@@ -234,18 +238,20 @@
             else:
                 gathered[...] += here
 
-    own_turn = {
-        "A": (hand_on, 0), "B": (hand_over, 1), "C": (own_experts, 2), "D": (add_pair, 3), "E": (add_all, 4),
-        "G": (gather, 6),
+    actions = {
+        "A": hand_on, "B": hand_over, "C": own_experts, "S": sibling_experts, "D": add_pair, "E": add_all, "G": gather,
     }
 
     prepare(0)
-    for load in loads[5:]:
-        load.wait()
     pl.semaphore_wait(barrier, 4 * n_tiles)
 
     @pl.loop(0, STEPS * period + OFFSET + 1)
     def _(turn):
+        @pl.when(turn == 1)
+        def _():
+            for load in loads[5:]:
+                load.wait()
+
         own = turn - 1 - c * OFFSET
         other = turn - 1 - (1 - c) * OFFSET
 
@@ -259,16 +265,12 @@
                 action(jnp.minimum(jnp.maximum(t, 0), STEPS - 1), jnp.minimum(jnp.maximum(q, 0), groups - 1))
 
         for name in ORDER:
-            if name == "S":
-                at_turn(sibling_experts, other, 2)
-            else:
-                action, delay = own_turn[name]
-                if name == "G":
-                    @pl.when((own >= 0) & (own < STEPS * period) & (own % period == 6))
-                    def _():
-                        meta(jnp.minimum(own // period, STEPS - 1), 2).wait_recv()
-
-                at_turn(action, own, delay)
+            if name == "G":
+                @pl.when((own >= 0) & (own < STEPS * period) & (own % period == TURN["G"]))
+                def _():
+                    meta(jnp.minimum(own // period, STEPS - 1), 2).wait_recv()
+
+            at_turn(actions[name], other if name == "S" else own, TURN[name])
 
         upcoming = (own + 1 + period) // period - 1
 
@@ -298,12 +300,8 @@
             def _():
                 land(t, k).wait_send()
 
-            to_home(t, k).wait_send()
-
-        @pl.loop(0, groups)
-        def _(q):
-            for copy in (to_sibling, to_partner, to_both, part_sibling, part_far, part_partner):
-                copy(t, q).wait_send()
+            for copy in (to_sibling, to_partner, to_both, part_sibling, part_far, part_partner, to_home):
+                copy(t, k).wait_send()
 
     store.wait()
 

time: 213 us -> 205 us (0.962)
  the two profiles are of different devices: /device:TPU:3 before, /device:TPU:41 now
where the time goes in v3:
time: 205 us
  Pallas kernels  203 us (99%)
    pallas_call x1, Pallas kernels, local(): pl.pallas_call(functools.partial(kernel, n_section, n_expert), out_shape=...  203 us

profile of v3, /device:TPU:41, one launch (start us, length us, event | category | flops | bytes accessed | tf_op | source)
XLA Modules:
  0.0 205.2 jit_solution(13059257174297688231)
XLA Ops:
  0.0 203.3 %shard_map.73 = bf16[1,128,2048]{2,1,0:T(8,128)(2,1)} custom-call(bf16[1,128,2048]{2,1,0:T(8,128)(2,1)} %x_ref.1, f32[1,2048]{1,0:T(1,128)} %gain_ref.1, bf16[1,8,2048]{2,1,0:T(8,128)(2,1)} %bitcast.1, bf16[1,1,2048,512]{3,2,1,0:T(8,128)(2,1)} %w_in_ref.1, bf16[1,1,256,2048]{3,2,1,0:T(8,128)(2,1)} %w_down_ref.1, s32[2,1,128]{2,1,0:T(1,128)} %ids_ref.1, ...), custom_call_target="tpu_custom_call" | custom-call | flops 5000000000 | bytes 5000000 | tf_op jit(solution)/shard_map/pallas_call | solution.py:316
  203.3 1.9 copy.9

commit v4 on v3

--- a/solution.py
+++ b/solution.py
@@ -9,8 +9,8 @@
 
 STEPS = 2
 PAIR = 2
-OFFSET = 5
-TURN = {"A": 0, "B": 1, "S": 2, "C": 2, "D": 3, "E": 5, "G": 7}
+OFFSET = 6
+TURN = {"A": 0, "B": 2, "S": 3, "C": 3, "D": 4, "E": 6, "G": 8}
 ORDER = "ADBSCEG"
 CAP = 24
 TOK = 128

time: 205 us -> 205 us (level)
  no operation moved by 1% of the time
where the time goes in v4:
time: 205 us
  Pallas kernels  203 us (99%)
    pallas_call x1, Pallas kernels, local(): pl.pallas_call(functools.partial(kernel, n_section, n_expert), out_shape=...  203 us

profile of v4, /device:TPU:41, one launch (start us, length us, event | category | flops | bytes accessed | tf_op | source)
XLA Modules:
  0.0 204.9 jit_solution(7877951692601858194)
XLA Ops:
  0.0 203.0 %shard_map.73 = bf16[1,128,2048]{2,1,0:T(8,128)(2,1)} custom-call(bf16[1,128,2048]{2,1,0:T(8,128)(2,1)} %x_ref.1, f32[1,2048]{1,0:T(1,128)} %gain_ref.1, bf16[1,8,2048]{2,1,0:T(8,128)(2,1)} %bitcast.1, bf16[1,1,2048,512]{3,2,1,0:T(8,128)(2,1)} %w_in_ref.1, bf16[1,1,256,2048]{3,2,1,0:T(8,128)(2,1)} %w_down_ref.1, s32[2,1,128]{2,1,0:T(1,128)} %ids_ref.1, ...), custom_call_target="tpu_custom_call" | custom-call | flops 5000000000 | bytes 5000000 | tf_op jit(solution)/shard_map/pallas_call | solution.py:316
  203.0 1.9 copy.9

commit v5 on v4

--- a/solution.py
+++ b/solution.py
@@ -9,7 +9,7 @@
 
 STEPS = 2
 PAIR = 2
-OFFSET = 6
+OFFSET = 7
 TURN = {"A": 0, "B": 2, "S": 3, "C": 3, "D": 4, "E": 6, "G": 8}
 ORDER = "ADBSCEG"
 CAP = 24

time: 205 us -> 213 us (1.039)
  the two profiles are of different devices: /device:TPU:41 before, /device:TPU:65 now
where the time goes in v5:
time: 213 us
  Pallas kernels  211 us (99%)
    pallas_call x1, Pallas kernels, local(): pl.pallas_call(functools.partial(kernel, n_section, n_expert), out_shape=...  211 us

profile of v5, /device:TPU:65, one launch (start us, length us, event | category | flops | bytes accessed | tf_op | source)
XLA Modules:
  0.0 213.1 jit_solution(16235865536782092284)
XLA Ops:
  0.0 211.2 %shard_map.73 = bf16[1,128,2048]{2,1,0:T(8,128)(2,1)} custom-call(bf16[1,128,2048]{2,1,0:T(8,128)(2,1)} %x_ref.1, f32[1,2048]{1,0:T(1,128)} %gain_ref.1, bf16[1,8,2048]{2,1,0:T(8,128)(2,1)} %bitcast.1, bf16[1,1,2048,512]{3,2,1,0:T(8,128)(2,1)} %w_in_ref.1, bf16[1,1,256,2048]{3,2,1,0:T(8,128)(2,1)} %w_down_ref.1, s32[2,1,128]{2,1,0:T(1,128)} %ids_ref.1, ...), custom_call_target="tpu_custom_call" | custom-call | flops 5000000000 | bytes 5000000 | tf_op jit(solution)/shard_map/pallas_call | solution.py:316
  211.2 1.9 copy.9
